TPU v7x, 32 devices: a whole 2x2x4 slice. The times are simulated.
32 devices in a mesh: kv: 2 (over core), page: 16 (over z, y, x).
Axes of the slice: x: 2, y: 2, z: 4, core: 2. Of those that a mesh axis runs over, the one named last changes fastest.
Arguments:
- tokens: bfloat16 [4096, 2048], P('page'), may hold values from -6 to 6
- in_gain: float32 [2048], replicated, may hold values from 0.4 to 1.6
- w_query: bfloat16 [2048, 2048], P(None, 'kv'), may hold values from -0.125 to 0.125
- key_projection_weight: bfloat16 [2048, 512], P(None, 'kv'), may hold values from -0.125 to 0.125
- value_projection_weight: bfloat16 [2048, 512], P(None, 'kv'), may hold values from -0.125 to 0.125
- q_gain: float32 [256], replicated, may hold values from 0.5 to 6
- k_gain: float32 [256], replicated, may hold values from 0.4 to 1.6
- w_out: bfloat16 [2048, 2048], P('kv'), may hold values from -0.125 to 0.125
- post_gain: float32 [2048], replicated, may hold values from 0.25 to 1.75
- laurel_left: bfloat16 [2048, 64], replicated, may hold values from -0.125 to 0.125
- laurel_right: bfloat16 [64, 2048], replicated, may hold values from -0.75 to 0.75
- laurel_gain: float32 [2048], replicated, may hold values from 0.25 to 1.75
- prefix_key_slots: bfloat16 [16384, 512], P('page', 'kv'), may hold values from -20 to 20
- prefix_value_slots: bfloat16 [16384, 512], P('page', 'kv'), may hold values from -6 to 6
- prefix_slot_map: int32 [128], replicated, may hold values from 0 to 127, each once
- page_lengths: int32 [8], replicated, may hold values from 1 to 8, 32 in all
- request_group: int32 [8], replicated, may hold values from 0 to 3
- suffix_page_map: int32 [32], P('page'), may hold values from 0 to 31, as said below
Outputs:
- layer_out: bfloat16 [4096, 2048], P('page', 'kv')
- suffix_key_cache: bfloat16 [4096, 512], P('page', 'kv')
- suffix_value_cache: bfloat16 [4096, 512], P('page', 'kv')
Inputs may be any that keep to these rules, and one draw needn't show every extreme that they name: `prefix_slot_map`: A permutation: entry g * 32 + j names the page slot (rows of 128 tokens of prefix_key_slots and prefix_value_slots) that holds page j of prefix g. `page_lengths`: they sum to 32; some request has exactly 8 pages. `suffix_page_map`: A permutation that keeps every logical page within the aligned block of 2 pages that contains it.
All inputs are finite; a program needn't handle non-finite values.
Results may differ from a plain program's by a relative error of at most 0.01.
The roundings to bfloat16 on the way count: a program that leaves them out, or rounds other values in their place, can miss the bound.
Values may be sent and summed in bfloat16 or wider, within the bound.
A program may use at most 128 MiB of HBM per device.

v0:
```python
import functools

import jax
import jax.numpy as jnp
from jax import lax
from jax.experimental import pallas as pl
from jax.experimental.pallas import tpu as pltpu
from jax.sharding import PartitionSpec as P

HEAD_SIZE = 256
PAGE_TOKENS = 128
PREFIX_TOKENS = 4096
PREFIX_COUNT = 4
MAXP = 8
PREFIX_PAGES = 32


epsilon = 1e-06
rope_base = 1000000.0
masked_low = -1e30


PLANE = 4
CHUNK = 512
MESH = pl.DeviceIdType.MESH
ANY = pl.BlockSpec(memory_space=pl.ANY)
VMEM_LIMIT = 56 * 1024 * 1024


def rms_scale(values):
    return lax.rsqrt(jnp.mean(values * values, axis=-1, keepdims=True) + epsilon)


def rotate(values, positions):
    half_dim = values.shape[-1] // 2
    inv_freq = rope_base ** (-(jnp.arange(half_dim).astype(jnp.float32) * 2.0 / values.shape[-1]))
    angles = positions.astype(jnp.float32)[:, None] * inv_freq[None, :]
    cosine = jnp.cos(angles)[:, None, :]
    sines = jnp.sin(angles)[:, None, :]
    first_half = values[..., :half_dim]
    second_half = values[..., half_dim:]
    return jnp.concatenate(
        [first_half * cosine - second_half * sines, second_half * cosine + first_half * sines],
        axis=-1,
    )


def project(
    tokens,
    in_gain,
    w_query,
    key_projection_weight,
    value_projection_weight,
    q_gain,
    k_gain,
    positions,
):
    tok_count = tokens.shape[0]
    tokens_wide = tokens.astype(jnp.float32)
    normed = (tokens_wide * rms_scale(tokens_wide) * in_gain).astype(jnp.bfloat16)
    queries = jnp.dot(normed, w_query, preferred_element_type=jnp.float32).reshape(
        tok_count, -1, HEAD_SIZE
    )
    queries = rotate(queries * rms_scale(queries) * q_gain, positions).astype(jnp.bfloat16)
    fresh_key_rows = jnp.dot(
        normed, key_projection_weight, preferred_element_type=jnp.float32
    ).reshape(tok_count, -1, HEAD_SIZE)
    fresh_key_rows = rotate(fresh_key_rows * rms_scale(fresh_key_rows) * k_gain, positions).astype(
        jnp.bfloat16
    )
    fresh_value_rows = jnp.dot(
        normed, value_projection_weight, preferred_element_type=jnp.float32
    ).reshape(tok_count, -1, HEAD_SIZE)
    fresh_value_rows = (fresh_value_rows * rms_scale(fresh_value_rows)).astype(jnp.bfloat16)
    return (
        normed,
        queries,
        fresh_key_rows.reshape(tok_count, HEAD_SIZE),
        fresh_value_rows.reshape(tok_count, HEAD_SIZE),
    )


def greet(devices):
    barrier = pltpu.get_barrier_semaphore()
    for device in devices:
        pl.semaphore_signal(barrier, inc=1, device_id={"page": device}, device_id_type=MESH)
    pl.semaphore_wait(barrier, len(devices))


def gather_kernel(
    blocks, pk, pv, fk, fv, q, pk_all, pv_all, fk_all, fv_all, q_all, local_sem, send, recv, q_send, q_recv
):
    me = lax.axis_index("page")
    mine = lax.rem(me, PLANE)
    block = lax.div(me, PLANE)
    slot_x = mine + 1 - 2 * lax.rem(mine, 2)
    slot_y = lax.rem(mine + 2, PLANE)
    slot_far = slot_x + slot_y - mine
    base = block * PLANE
    peers = [lax.rem(block + d, blocks) * PLANE + mine for d in range(1, blocks)]
    greet([base + slot_x, base + slot_y, *peers])
    own = [(pk, pk_all), (fk, fk_all), (pv, pv_all), (fv, fv_all)]

    def copy(kind, source, slot, to, lane):
        return pltpu.make_async_remote_copy(
            src_ref=source,
            dst_ref=own[kind][1].at[slot],
            send_sem=send.at[kind, lane],
            recv_sem=recv.at[kind, slot],
            device_id={"page": base + to},
            device_id_type=MESH,
        )

    started = []

    def begin(made):
        made.start()
        started.append(made)

    for kind in (0, 1):
        begin(copy(kind, own[kind][0], mine, slot_x, 0))
    for kind in (2, 3):
        begin(copy(kind, own[kind][0], mine, slot_y, 1))
    arriving = []
    for d in range(1, blocks):
        to = lax.rem(block + d, blocks) * PLANE + mine
        begin(
            pltpu.make_async_remote_copy(
                src_ref=q,
                dst_ref=q_all.at[block],
                send_sem=q_send.at[d - 1],
                recv_sem=q_recv.at[d - 1],
                device_id={"page": to},
                device_id_type=MESH,
            )
        )
        arriving.append(
            pltpu.make_async_remote_copy(
                src_ref=q,
                dst_ref=q_all.at[lax.rem(block + blocks - d, blocks)],
                send_sem=q_send.at[d - 1],
                recv_sem=q_recv.at[d - 1],
                device_id={"page": to},
                device_id_type=MESH,
            )
        )
    for kind in (2, 3):
        begin(copy(kind, own[kind][0], mine, slot_x, 0))
    for kind in (0, 1):
        begin(copy(kind, own[kind][0], mine, slot_y, 1))
    locals_ = [
        pltpu.make_async_copy(source, whole.at[mine], local_sem.at[n])
        for n, (source, whole) in enumerate(own)
    ]
    locals_.append(pltpu.make_async_copy(q, q_all.at[block], local_sem.at[4]))
    for made in locals_:
        made.start()
    for kind in (0, 1, 2, 3):
        near, to, lane = (slot_x, slot_y, 2) if kind < 2 else (slot_y, slot_x, 2)
        copy(kind, own[kind][0], near, to, lane).wait_recv()
        begin(copy(kind, own[kind][1].at[near], near, to, lane))
    for kind in (0, 1, 2, 3):
        other = slot_y if kind < 2 else slot_x
        copy(kind, own[kind][0], other, other, 0).wait_recv()
        copy(kind, own[kind][0], slot_far, other, 0).wait_recv()
    for made in arriving:
        made.wait_recv()
    for made in started:
        made.wait_send()
    for made in locals_:
        made.wait()


def gather(pk, pv, fk, fv, q, blocks):
    def many(source, n):
        return jax.ShapeDtypeStruct((n, *source.shape), source.dtype)

    return pl.pallas_call(
        functools.partial(gather_kernel, blocks),
        out_shape=[many(pk, PLANE), many(pv, PLANE), many(fk, PLANE), many(fv, PLANE), many(q, blocks)],
        in_specs=[ANY] * 5,
        out_specs=[ANY] * 5,
        scratch_shapes=[
            pltpu.SemaphoreType.DMA((5,)),
            pltpu.SemaphoreType.DMA((4, 3)),
            pltpu.SemaphoreType.DMA((4, PLANE)),
            pltpu.SemaphoreType.DMA((blocks - 1,)),
            pltpu.SemaphoreType.DMA((blocks - 1,)),
        ],
        compiler_params=pltpu.CompilerParams(collective_id=0, has_side_effects=True),
    )(pk, pv, fk, fv, q)


def attend_kernel(
    slots, places, info, pk, pv, fk, fv, q_ref, out_ref, stat_ref, keys, values, top, total, mixed, sem
):
    step = pl.program_id(0)
    prefix_rows = slots * PAGE_TOKENS
    suffix_rows = fk.shape[0]

    @pl.when(step == 0)
    def _():
        values[prefix_rows + suffix_rows :, :] = jnp.zeros((CHUNK, HEAD_SIZE), jnp.bfloat16)
        moves = [
            pltpu.make_async_copy(fk, keys.at[pl.ds(prefix_rows, suffix_rows), :], sem.at[2 * slots]),
            pltpu.make_async_copy(
                fv, values.at[pl.ds(prefix_rows, suffix_rows), :], sem.at[2 * slots + 1]
            ),
        ]
        for n in range(slots):
            source = pl.ds(n * PAGE_TOKENS, PAGE_TOKENS)
            there = pl.ds(pl.multiple_of(places[n] * PAGE_TOKENS, PAGE_TOKENS), PAGE_TOKENS)
            moves.append(pltpu.make_async_copy(pk.at[source, :], keys.at[there, :], sem.at[n]))
            moves.append(
                pltpu.make_async_copy(pv.at[source, :], values.at[there, :], sem.at[slots + n])
            )
        for move in moves:
            move.start()
        for move in moves:
            move.wait()

    top[...] = jnp.full_like(top, masked_low)
    total[...] = jnp.zeros_like(total)
    mixed[...] = jnp.zeros_like(mixed)
    rows = q_ref.shape[1]
    prefix_low, prefix_high = info[step * 8], info[step * 8 + 1]
    suffix_low, suffix_high = info[step * 8 + 2], info[step * 8 + 3]
    first_token = info[step * 8 + 4]

    def fold(offset, valid):
        offset = pl.multiple_of(offset, PAGE_TOKENS)
        scores = lax.dot_general(
            keys[pl.ds(offset, CHUNK), :],
            q_ref[0],
            (((1,), (1,)), ((), ())),
            preferred_element_type=jnp.float32,
        )
        scores = jnp.where(valid, scores, masked_low)
        row_top = jnp.maximum(top[...], jnp.max(scores, axis=0, keepdims=True))
        factor = jnp.exp(top[...] - row_top)
        weights = jnp.exp(scores - row_top)
        total[...] = total[...] * factor + jnp.sum(weights, axis=0, keepdims=True)
        mixed[...] = mixed[...] * factor + lax.dot_general(
            values[pl.ds(offset, CHUNK), :],
            weights.astype(jnp.bfloat16),
            (((0,), (0,)), ((), ())),
            preferred_element_type=jnp.float32,
        )
        top[...] = row_top

    in_chunk = lax.broadcasted_iota(jnp.int32, (CHUNK, rows), 0)
    token = lax.rem(lax.broadcasted_iota(jnp.int32, (CHUNK, rows), 1), PAGE_TOKENS)
    chunk_pages = CHUNK // PAGE_TOKENS

    def prefix_step(n, _):
        start = (prefix_low + n * chunk_pages) * PAGE_TOKENS
        fold(start, in_chunk < prefix_high * PAGE_TOKENS - start)
        return 0

    def suffix_step(n, _):
        start = (suffix_low + n * chunk_pages) * PAGE_TOKENS
        valid = (in_chunk < suffix_high * PAGE_TOKENS - start) & (
            in_chunk - token <= first_token - start
        )
        fold(start + prefix_rows, valid)
        return 0

    lax.fori_loop(0, lax.div(prefix_high - prefix_low + chunk_pages - 1, chunk_pages), prefix_step, 0)
    lax.fori_loop(0, lax.div(suffix_high - suffix_low + chunk_pages - 1, chunk_pages), suffix_step, 0)
    scale = jnp.where(total[...] > 0, 1.0 / jnp.maximum(total[...], 1e-30), 0.0)
    out_ref[0] = (mixed[...] * scale).astype(jnp.bfloat16)
    stat_ref[0, 0:1, :] = top[...]
    stat_ref[0, 1:2, :] = total[...]
    stat_ref[0, 2:8, :] = jnp.zeros((6, rows), jnp.float32)


def attend(places, info, pk, pv, fk, fv, queries):
    pages, rows, _ = queries.shape
    slots = places.shape[0]
    span = pk.shape[0] + fk.shape[0] + CHUNK
    return pl.pallas_call(
        functools.partial(attend_kernel, slots),
        out_shape=[
            jax.ShapeDtypeStruct((pages, HEAD_SIZE, rows), jnp.bfloat16),
            jax.ShapeDtypeStruct((pages, 8, rows), jnp.float32),
        ],
        grid_spec=pltpu.PrefetchScalarGridSpec(
            num_scalar_prefetch=2,
            grid=(pages,),
            in_specs=[ANY] * 4 + [pl.BlockSpec((1, rows, HEAD_SIZE), lambda i, *_: (i, 0, 0))],
            out_specs=[
                pl.BlockSpec((1, HEAD_SIZE, rows), lambda i, *_: (i, 0, 0)),
                pl.BlockSpec((1, 8, rows), lambda i, *_: (i, 0, 0)),
            ],
            scratch_shapes=[
                pltpu.VMEM((span, HEAD_SIZE), jnp.bfloat16),
                pltpu.VMEM((span, HEAD_SIZE), jnp.bfloat16),
                pltpu.VMEM((1, rows), jnp.float32),
                pltpu.VMEM((1, rows), jnp.float32),
                pltpu.VMEM((HEAD_SIZE, rows), jnp.float32),
                pltpu.SemaphoreType.DMA((2 * slots + 2,)),
            ],
        ),
        compiler_params=pltpu.CompilerParams(vmem_limit_bytes=VMEM_LIMIT),
    )(places, info, pk, pv, fk, fv, queries)


def send_back_kernel(blocks, out, stat, out_all, stat_all, local_sem, send, recv):
    me = lax.axis_index("page")
    mine = lax.rem(me, PLANE)
    block = lax.div(me, PLANE)
    greet([lax.rem(block + d, blocks) * PLANE + mine for d in range(1, blocks)])
    started = []
    arriving = []
    for d in range(1, blocks):
        other = lax.rem(block + d, blocks)
        for n, (source, whole) in enumerate(((out, out_all), (stat, stat_all))):
            for slot, made in ((block, started), (lax.rem(block + blocks - d, blocks), arriving)):
                made.append(
                    pltpu.make_async_remote_copy(
                        src_ref=source.at[other],
                        dst_ref=whole.at[slot],
                        send_sem=send.at[n, d - 1],
                        recv_sem=recv.at[n, d - 1],
                        device_id={"page": other * PLANE + mine},
                        device_id_type=MESH,
                    )
                )
            started[-1].start()
    own = [
        pltpu.make_async_copy(out.at[block], out_all.at[block], local_sem.at[0]),
        pltpu.make_async_copy(stat.at[block], stat_all.at[block], local_sem.at[1]),
    ]
    for made in own:
        made.start()
    for made in arriving:
        made.wait_recv()
    for made in started:
        made.wait_send()
    for made in own:
        made.wait()


def send_back(out, stat):
    blocks = out.shape[0]
    return pl.pallas_call(
        functools.partial(send_back_kernel, blocks),
        out_shape=[
            jax.ShapeDtypeStruct(out.shape, out.dtype),
            jax.ShapeDtypeStruct(stat.shape, stat.dtype),
        ],
        in_specs=[ANY] * 2,
        out_specs=[ANY] * 2,
        scratch_shapes=[
            pltpu.SemaphoreType.DMA((2,)),
            pltpu.SemaphoreType.DMA((2, blocks - 1)),
            pltpu.SemaphoreType.DMA((2, blocks - 1)),
        ],
        compiler_params=pltpu.CompilerParams(collective_id=1, has_side_effects=True),
    )(out, stat)


def page_facts(pages, page_lengths, request_group):
    ids = jnp.arange(page_lengths.shape[0])
    starts = jnp.sum(jnp.where(ids[None, :] < ids[:, None], page_lengths[None, :], 0), axis=1)
    belongs = (pages[:, None] >= starts[None, :]) & (
        pages[:, None] < (starts + page_lengths)[None, :]
    )
    first = jnp.sum(jnp.where(belongs, starts[None, :], 0), axis=1)
    group = jnp.sum(jnp.where(belongs, request_group[None, :], 0), axis=1)
    return first, group


def local(
    tokens,
    in_gain,
    w_query,
    key_projection_weight,
    value_projection_weight,
    q_gain,
    k_gain,
    w_out,
    post_gain,
    laurel_left,
    laurel_right,
    laurel_gain,
    prefix_key_slots,
    prefix_value_slots,
    prefix_slot_map,
    page_lengths,
    request_group,
    suffix_page_map,
):
    tok_count, model_width = tokens.shape
    pages_here = tok_count // PAGE_TOKENS
    device = lax.axis_index("page")
    blocks = lax.axis_size("page") // PLANE
    mine = device % PLANE
    block = device // PLANE
    heads = w_query.shape[1] // HEAD_SIZE
    plane_pages = PLANE * pages_here

    my_pages = device * pages_here + jnp.arange(pages_here, dtype=jnp.int32)
    my_first, _ = page_facts(my_pages, page_lengths, request_group)
    position = (
        (my_pages - my_first)[:, None] * PAGE_TOKENS + jnp.arange(PAGE_TOKENS, dtype=jnp.int32)
    ).reshape(tok_count)
    normed, queries, fresh_key_rows, fresh_value_rows = project(
        tokens,
        in_gain,
        w_query,
        key_projection_weight,
        value_projection_weight,
        q_gain,
        k_gain,
        position + PREFIX_TOKENS,
    )
    local_slot = suffix_page_map - device * pages_here

    def place(rows):
        paged = rows.reshape(pages_here, PAGE_TOKENS, HEAD_SIZE)
        parts = []
        for slot in range(pages_here):
            part = paged[0]
            for n in range(1, pages_here):
                part = jnp.where(local_slot[n] == slot, paged[n], part)
            parts.append(part)
        return jnp.concatenate(parts, axis=0)

    suffix_key_cache = place(fresh_key_rows)
    suffix_value_cache = place(fresh_value_rows)

    slots = PLANE * prefix_key_slots.shape[0] // PAGE_TOKENS
    slot_ids = block * slots + jnp.arange(slots, dtype=jnp.int32)
    map_group = jnp.arange(prefix_slot_map.shape[0], dtype=jnp.int32) // PREFIX_PAGES
    slot_group = jnp.sum(
        jnp.where(slot_ids[:, None] == prefix_slot_map[None, :], map_group[None, :], 0), axis=1
    )
    order = jnp.arange(slots, dtype=jnp.int32)
    ahead = (slot_group[None, :] < slot_group[:, None]) | (
        (slot_group[None, :] == slot_group[:, None]) & (order[None, :] < order[:, None])
    )
    places = jnp.sum(ahead.astype(jnp.int32), axis=1)
    q_pages = (
        (jnp.arange(blocks, dtype=jnp.int32) * PLANE + mine)[:, None] * pages_here
        + jnp.arange(pages_here, dtype=jnp.int32)
    ).reshape(-1)
    q_first, q_group = page_facts(q_pages, page_lengths, request_group)
    prefix_low = jnp.sum((slot_group[None, :] < q_group[:, None]).astype(jnp.int32), axis=1)
    prefix_high = jnp.sum((slot_group[None, :] <= q_group[:, None]).astype(jnp.int32), axis=1)
    plane_first = block * plane_pages
    suffix_low = jnp.maximum(q_first - plane_first, 0)
    suffix_high = jnp.minimum(q_pages + 1 - plane_first, plane_pages)
    suffix_low = jnp.minimum(suffix_low, plane_pages)
    suffix_high = jnp.maximum(suffix_high, suffix_low)
    first_token = (q_pages - plane_first) * PAGE_TOKENS
    nothing = jnp.zeros_like(first_token)
    info = jnp.stack(
        [prefix_low, prefix_high, suffix_low, suffix_high, first_token, nothing, nothing, nothing],
        axis=1,
    ).reshape(-1)

    paged_queries = queries.reshape(pages_here, PAGE_TOKENS, heads, HEAD_SIZE).transpose(0, 2, 1, 3)
    paged_queries = paged_queries.reshape(pages_here * heads * PAGE_TOKENS, HEAD_SIZE)
    pk, pv, fk, fv, q_all = gather(
        prefix_key_slots, prefix_value_slots, fresh_key_rows, fresh_value_rows, paged_queries, blocks
    )
    out, stat = attend(
        places,
        info,
        pk.reshape(-1, HEAD_SIZE),
        pv.reshape(-1, HEAD_SIZE),
        fk.reshape(-1, HEAD_SIZE),
        fv.reshape(-1, HEAD_SIZE),
        q_all.reshape(blocks * pages_here, heads * PAGE_TOKENS, HEAD_SIZE),
    )
    out, stat = send_back(
        out.reshape(blocks, pages_here, HEAD_SIZE, -1), stat.reshape(blocks, pages_here, 8, -1)
    )
    tops, totals = stat[:, :, 0, :], stat[:, :, 1, :]
    share = totals * jnp.exp(tops - jnp.max(tops, axis=0, keepdims=True))
    share = share / jnp.sum(share, axis=0, keepdims=True)
    attended = jnp.sum(out.astype(jnp.float32) * share[:, :, None, :], axis=0).astype(jnp.bfloat16)
    attended = (
        attended.reshape(pages_here, HEAD_SIZE, heads, PAGE_TOKENS)
        .transpose(0, 3, 2, 1)
        .reshape(tok_count, heads * HEAD_SIZE)
    )
    attn_part = jnp.dot(attended, w_out, preferred_element_type=jnp.float32).astype(jnp.bfloat16)
    other_part = lax.ppermute(attn_part, "kv", [(0, 1), (1, 0)])
    summed_out = attn_part.astype(jnp.float32) + other_part.astype(jnp.float32)
    kv_index = lax.axis_index("kv")
    half_width = model_width // lax.axis_size("kv")

    def columns(source):
        return lax.dynamic_slice_in_dim(source, kv_index * half_width, half_width, source.ndim - 1)

    low_rank = jnp.dot(normed, laurel_left, preferred_element_type=jnp.float32).astype(jnp.bfloat16)
    laurel_full = jnp.dot(low_rank, laurel_right, preferred_element_type=jnp.float32)
    laurel_part = columns(laurel_full) * rms_scale(laurel_full) * columns(laurel_gain)
    laurel = columns(normed).astype(jnp.float32) + laurel_part
    attn_branch = columns(summed_out) * rms_scale(summed_out) * columns(post_gain)
    layer_out = (
        (columns(tokens).astype(jnp.float32) + attn_branch + laurel) * 2.0 ** (-0.5)
    ).astype(jnp.bfloat16)
    return (layer_out, suffix_key_cache, suffix_value_cache)


def solution(mesh):
    placed = (
        P("page", None),
        P(),
        P(None, "kv"),
        P(None, "kv"),
        P(None, "kv"),
        P(),
        P(),
        P("kv", None),
        P(),
        P(),
        P(),
        P(),
        P("page", "kv"),
        P("page", "kv"),
        P(),
        P(),
        P(),
        P("page"),
    )
    return jax.shard_map(
        local,
        mesh=mesh,
        in_specs=placed,
        out_specs=(P("page", "kv"), P("page", "kv"), P("page", "kv")),
        check_vma=False,
    )
```

profile of v0, /device:TPU:13, one launch (start us, length us, event | category | flops | bytes accessed | tf_op | source)
XLA Modules:
  0.0 179.0 jit_solution(148611048236108175)
XLA Ops:
  0.9 0.8 select_reduce_fusion.3
  2.5 0.9 select_reduce_fusion.1
  3.5 0.8 select_reduce_fusion
  4.3 0.7 convert_reduce_fusion.places
  7.2 1.5 fusion
  8.7 1.5 fusion.2
  10.2 4.4 %fusion.25 = f32[256,1024]{1,0:T(8,128)} fusion(bf16[256,2048]{1,0:T(8,128)(2,1)S(1)} %fusion.2, bf16[2048,1024]{1,0:T(8,128)(2,1)} %param.20), kind=kOutput, calls=%fused_computation.92 | convolution fusion | flops 1073741824 | bytes 6291456 | tf_op jit(solution)/shard_map/dot_general | solution.py:61
  14.7 1.7 reshape.428
  17.4 1.4 fusion.4
  19.0 0.8 copy.84
  20.4 0.8 copy.81
  21.2 1.1 multiply_bitcast_fusion
  24.1 0.8 multiply_convert_fusion.1.fv
  24.9 59.4 %shard_map.193 = (bf16[4,1024,256]{2,1,0:T(8,128)(2,1)}, bf16[4,1024,256]{2,1,0:T(8,128)(2,1)}, bf16[4,256,256]{2,1,0:T(8,128)(2,1)}, bf16[4,256,256]{2,1,0:T(8,128)(2,1)}, bf16[4,1024,256]{2,1,0:T(8,128)(2,1)}) custom-call(bf16[1024,256]{1,0:T(8,128)(2,1)} %pk.1, bf16[1024,256]{1,0:T(8,128)(2,1)} %pv.1, bf16[256,256]{1,0:T(8,128)(2,1)} %pad_maximum_fusion.fk, ...), custom_call_target="tpu_custom_call" | custom-call | tf_op jit(solution)/shard_map/pallas_call | solution.py:178
  84.2 22.9 %shard_map.194 = (bf16[8,256,512]{2,1,0:T(8,128)(2,1)}, f32[8,8,512]{2,1,0:T(8,128)}) custom-call(s32[32]{0:T(128)} %convert_reduce_fusion.places, s32[64]{0:T(128)} %reshape.427.info, bf16[4096,256]{1,0:T(8,128)(2,1)} %bitcast.70, bf16[4096,256]{1,0:T(8,128)(2,1)} %bitcast.71, bf16[1024,256]{1,0:T(8,128)(2,1)} %bitcast.78, bf16[1024,256]{1,0:T(8,128)(2,1)} %bitcast.79, ...), custom_call_target="tpu_custom_call" | custom-call | tf_op jit(solution)/shard_map/pallas_call | solution.py:281
  107.1 51.7 %shard_map.195 = (bf16[4,2,256,512]{3,2,1,0:T(8,128)(2,1)}, f32[4,2,8,512]{3,2,1,0:T(8,128)}) custom-call(bf16[4,2,256,512]{3,2,1,0:T(8,128)(2,1)} %bitcast.67, f32[4,2,8,512]{3,2,1,0:T(8,128)} %bitcast.80), custom_call_target="tpu_custom_call" | custom-call | tf_op jit(solution)/shard_map/pallas_call | solution.py:346
  158.9 1.0 copy.85
  159.9 0.9 slice_reduce_fusion
  160.9 2.0 %multiply_reduce_fusion = bf16[2,256,512]{2,1,0:T(8,128)(2,1)S(1)} fusion(bf16[4,2,256,512]{3,2,1,0:T(8,128)(2,1)} %get-tuple-element.19, f32[4,2,512]{2,1,0:T(2,128)S(1)} %fusion.20), kind=kLoop, calls=%fused_computation | loop fusion | flops 2883584 | bytes 2637824 | tf_op jit(solution)/shard_map/reduce_sum | solution.py:483
  163.6 3.5 %convolution_convert_fusion = bf16[256,2048]{1,0:T(8,128)(2,1)S(1)} fusion(bf16[256,1024]{1,0:T(8,128)(2,1)S(1)} %bitcast.77, bf16[1024,2048]{1,0:T(8,128)(2,1)} %param.25), kind=kOutput, calls=%fused_computation.3 | convolution fusion | flops 1074266112 | bytes 5767168 | tf_op jit(solution)/shard_map/dot_general | solution.py:489
  167.1 1.3 collective-permute-start
  171.8 3.8 %multiply_reduce_fusion.1 = (f32[256]{0:T(256)S(1)}, f32[256,2048]{1,0:T(8,128)}) fusion(bf16[64,2048]{1,0:T(8,128)(2,1)} %param.28, bf16[256,2048]{1,0:T(8,128)(2,1)S(1)} %fusion.2, bf16[2048,64]{0,1:T(8,128)(2,1)} %param.27), kind=kOutput, calls=%fused_computation.7 | convolution fusion | flops 135282432 | bytes 3671040 | tf_op jit(solution)/shard_map/dot_general | solution.py:499
  175.6 1.8 %multiply_reduce_fusion.2 = (f32[256]{0:T(256)S(1)}, f32[256,2048]{1,0:T(8,128)S(1)}) fusion(bf16[256,2048]{1,0:T(8,128)(2,1)} %collective-permute-done, bf16[256,2048]{1,0:T(8,128)(2,1)S(1)} %convolution_convert_fusion), kind=kLoop, calls=%fused_computation.8 | loop fusion | flops 2621184 | bytes 4195328 | tf_op jit(solution)/shard_map/reduce_sum | solution.py:31
  177.8 1.2 multiply_convert_fusion
  (67 shorter events, 9.9 us)
Async XLA Ops:
  0.6 19.2 %copy-start = (bf16[2048,256]{1,0:T(8,128)(2,1)S(1)}, bf16[2048,256]{1,0:T(8,128)(2,1)}, u32[]{:S(2)}) copy-start(bf16[2048,256]{1,0:T(8,128)(2,1)} %param.21) | copy-start | bytes 3145732
  14.7 2.7 %copy-start.5 = (f32[256]{0:T(256)S(1)}, f32[256]{0:T(256)}, u32[]{:S(2)}) copy-start(f32[256]{0:T(256)} %param.23) | copy-start | bytes 3076
  19.0 2.2 %copy-start.6 = (f32[256]{0:T(256)S(1)}, f32[256]{0:T(256)}, u32[]{:S(2)}) copy-start(f32[256]{0:T(256)} %param.24) | copy-start | bytes 3076
  19.9 3.0 %copy-start.4 = (bf16[2048,256]{1,0:T(8,128)(2,1)S(1)}, bf16[2048,256]{1,0:T(8,128)(2,1)}, u32[]{:S(2)}) copy-start(bf16[2048,256]{1,0:T(8,128)(2,1)} %param.22) | copy-start | bytes 3145732
  163.6 7.4 %copy-start.3 = (bf16[256,256]{1,0:T(8,128)(2,1)S(1)}, bf16[256,256]{1,0:T(8,128)(2,1)}, u32[]{:S(2)}) copy-start(bf16[256,256]{1,0:T(8,128)(2,1)} %multiply_convert_fusion.1.fv) | copy-start | bytes 393220
  167.1 8.4 %collective-permute-start = (bf16[256,2048]{1,0:T(8,128)(2,1)S(1)}, bf16[256,2048]{1,0:T(8,128)(2,1)}, u32[]{:S(2)}, u32[]{:S(2)}) collective-permute-start(bf16[256,2048]{1,0:T(8,128)(2,1)S(1)} %convolution_convert_fusion), channel_id=1, source_target_pairs={{0,16},{16,0},{1,17},{17,1},{2,18},{18,2},{3,19},{19,3},{4,20},{20... | collective-permute-start | bytes 3145736 | tf_op jit(solution)/shard_map/ppermute | solution.py:490
  175.5 1.9 %copy-start.1 = (bf16[256,2048]{1,0:T(8,128)(2,1)S(1)}, bf16[256,2048]{1,0:T(8,128)(2,1)}, u32[]{:S(2)}) copy-start(bf16[256,2048]{1,0:T(8,128)(2,1)} %param.18) | copy-start | bytes 3145732
  175.5 2.2 %copy-start.2 = (f32[256,2048]{1,0:T(8,128)S(1)}, f32[256,2048]{1,0:T(8,128)}, u32[]{:S(2)}) copy-start(f32[256,2048]{1,0:T(8,128)} %get-tuple-element.49) | copy-start | bytes 6291460
  175.5 2.2 %dynamic-slice-start = ((f32[2048]{0:T(1024)}, s32[]{:T(128)}), f32[1024]{0:T(1024)S(1)}, s32[]{:S(2)}) async-start(f32[2048]{0:T(1024)} %param.26, s32[]{:T(128)} %select_n.79), calls=%async_computation | async-start | bytes 8704 | tf_op jit(solution)/shard_map/dynamic_slice | solution.py:496
  175.6 2.2 %dynamic-slice-start.1 = ((f32[2048]{0:T(1024)}, s32[]{:T(128)}), f32[1024]{0:T(1024)S(1)}, s32[]{:S(2)}) async-start(f32[2048]{0:T(1024)} %param.29, s32[]{:T(128)} %select_n.79), calls=%async_computation.1 | async-start | bytes 8704 | tf_op jit(solution)/shard_map/dynamic_slice | solution.py:496
where the time goes:
time: 183 us; the launch traced here: 179 us
  Pallas kernels  134 us (73%)
  other arithmetic  21.2 us (12%)
  matrix products  12.7 us (7%)
  local copies, waits for them, and re-layouts  7.49 us (4%)
  between operations  2.24 us (1%)
    pallas_call x1, Pallas kernels, gather(): pl.pallas_call(functools.partial(gather_kernel, blocks), out_shape=[many(...  59.4 us
    pallas_call x1, Pallas kernels, send_back(): pl.pallas_call(functools.partial(send_back_kernel, blocks), out_shape=[ja...  51.7 us
    pallas_call x1, Pallas kernels, attend(): pl.pallas_call(functools.partial(attend_kernel, slots), out_shape=[jax.Sh...  22.9 us
    dot_general x1, matrix products, project(): jnp.dot(normed, w_query, preferred_element_type=jnp.float32)  4.43 us
    dot_general x1, matrix products, local(): jnp.dot(low_rank, laurel_right, preferred_element_type=jnp.float32)  3.76 us
  transfers between devices with their start and end apart: 1, of which 0 were waited for; matrix products, arithmetic and copies ran while one was open for 3% of the time, Pallas kernels for 0%

commit v1 on v0

--- a/solution.py
+++ b/solution.py
@@ -87,133 +87,108 @@
     pl.semaphore_wait(barrier, len(devices))
 
 
-def gather_kernel(
-    blocks, pk, pv, fk, fv, q, pk_all, pv_all, fk_all, fv_all, q_all, local_sem, send, recv, q_send, q_recv
-):
+def gather_kernel(blocks, fresh, q, fresh_all, q_all, local_sem, send, recv, q_send, q_recv):
     me = lax.axis_index("page")
     mine = lax.rem(me, PLANE)
     block = lax.div(me, PLANE)
-    slot_x = mine + 1 - 2 * lax.rem(mine, 2)
-    slot_y = lax.rem(mine + 2, PLANE)
-    slot_far = slot_x + slot_y - mine
     base = block * PLANE
-    peers = [lax.rem(block + d, blocks) * PLANE + mine for d in range(1, blocks)]
-    greet([base + slot_x, base + slot_y, *peers])
-    own = [(pk, pk_all), (fk, fk_all), (pv, pv_all), (fv, fv_all)]
-
-    def copy(kind, source, slot, to, lane):
-        return pltpu.make_async_remote_copy(
-            src_ref=source,
-            dst_ref=own[kind][1].at[slot],
-            send_sem=send.at[kind, lane],
-            recv_sem=recv.at[kind, slot],
-            device_id={"page": base + to},
+    z_peers = [lax.rem(block + d, blocks) * PLANE + mine for d in range(1, blocks)]
+    peers = [base + lax.rem(mine + d, PLANE) for d in range(1, PLANE)]
+    greet([*z_peers, *peers])
+    started = []
+    for d in range(1, blocks):
+        started.append(
+            pltpu.make_async_remote_copy(
+                src_ref=q,
+                dst_ref=q_all.at[d],
+                send_sem=q_send.at[d - 1],
+                recv_sem=q_recv.at[d - 1],
+                device_id={"page": z_peers[d - 1]},
+                device_id_type=MESH,
+            )
+        )
+        started[-1].start()
+    for d in range(1, PLANE):
+        made = pltpu.make_async_remote_copy(
+            src_ref=fresh,
+            dst_ref=fresh_all.at[mine],
+            send_sem=send.at[d - 1],
+            recv_sem=recv.at[d - 1],
+            device_id={"page": peers[d - 1]},
             device_id_type=MESH,
         )
-
-    started = []
-
-    def begin(made):
         made.start()
         started.append(made)
-
-    for kind in (0, 1):
-        begin(copy(kind, own[kind][0], mine, slot_x, 0))
-    for kind in (2, 3):
-        begin(copy(kind, own[kind][0], mine, slot_y, 1))
-    arriving = []
-    for d in range(1, blocks):
-        to = lax.rem(block + d, blocks) * PLANE + mine
-        begin(
-            pltpu.make_async_remote_copy(
-                src_ref=q,
-                dst_ref=q_all.at[block],
-                send_sem=q_send.at[d - 1],
-                recv_sem=q_recv.at[d - 1],
-                device_id={"page": to},
-                device_id_type=MESH,
-            )
-        )
-        arriving.append(
-            pltpu.make_async_remote_copy(
-                src_ref=q,
-                dst_ref=q_all.at[lax.rem(block + blocks - d, blocks)],
-                send_sem=q_send.at[d - 1],
-                recv_sem=q_recv.at[d - 1],
-                device_id={"page": to},
-                device_id_type=MESH,
-            )
-        )
-    for kind in (2, 3):
-        begin(copy(kind, own[kind][0], mine, slot_x, 0))
-    for kind in (0, 1):
-        begin(copy(kind, own[kind][0], mine, slot_y, 1))
-    locals_ = [
-        pltpu.make_async_copy(source, whole.at[mine], local_sem.at[n])
-        for n, (source, whole) in enumerate(own)
+    own = [
+        pltpu.make_async_copy(fresh, fresh_all.at[mine], local_sem.at[0]),
+        pltpu.make_async_copy(q, q_all.at[0], local_sem.at[1]),
     ]
-    locals_.append(pltpu.make_async_copy(q, q_all.at[block], local_sem.at[4]))
-    for made in locals_:
+    for made in own:
         made.start()
-    for kind in (0, 1, 2, 3):
-        near, to, lane = (slot_x, slot_y, 2) if kind < 2 else (slot_y, slot_x, 2)
-        copy(kind, own[kind][0], near, to, lane).wait_recv()
-        begin(copy(kind, own[kind][1].at[near], near, to, lane))
-    for kind in (0, 1, 2, 3):
-        other = slot_y if kind < 2 else slot_x
-        copy(kind, own[kind][0], other, other, 0).wait_recv()
-        copy(kind, own[kind][0], slot_far, other, 0).wait_recv()
-    for made in arriving:
+    for made in started[: blocks - 1]:
         made.wait_recv()
+    for d in range(1, PLANE):
+        pltpu.make_async_remote_copy(
+            src_ref=fresh,
+            dst_ref=fresh_all.at[lax.rem(mine + PLANE - d, PLANE)],
+            send_sem=send.at[d - 1],
+            recv_sem=recv.at[d - 1],
+            device_id={"page": peers[d - 1]},
+            device_id_type=MESH,
+        ).wait_recv()
     for made in started:
         made.wait_send()
-    for made in locals_:
+    for made in own:
         made.wait()
 
 
-def gather(pk, pv, fk, fv, q, blocks):
-    def many(source, n):
-        return jax.ShapeDtypeStruct((n, *source.shape), source.dtype)
-
+def gather(fresh, q, blocks):
     return pl.pallas_call(
         functools.partial(gather_kernel, blocks),
-        out_shape=[many(pk, PLANE), many(pv, PLANE), many(fk, PLANE), many(fv, PLANE), many(q, blocks)],
-        in_specs=[ANY] * 5,
-        out_specs=[ANY] * 5,
+        out_shape=[
+            jax.ShapeDtypeStruct((PLANE, *fresh.shape), fresh.dtype),
+            jax.ShapeDtypeStruct((blocks, *q.shape), q.dtype),
+        ],
+        in_specs=[ANY] * 2,
+        out_specs=[ANY] * 2,
         scratch_shapes=[
-            pltpu.SemaphoreType.DMA((5,)),
-            pltpu.SemaphoreType.DMA((4, 3)),
-            pltpu.SemaphoreType.DMA((4, PLANE)),
+            pltpu.SemaphoreType.DMA((2,)),
+            pltpu.SemaphoreType.DMA((PLANE - 1,)),
+            pltpu.SemaphoreType.DMA((PLANE - 1,)),
             pltpu.SemaphoreType.DMA((blocks - 1,)),
             pltpu.SemaphoreType.DMA((blocks - 1,)),
         ],
         compiler_params=pltpu.CompilerParams(collective_id=0, has_side_effects=True),
-    )(pk, pv, fk, fv, q)
+        cost_estimate=pl.CostEstimate(flops=40 * 10**9, bytes_accessed=10**6, transcendentals=0),
+    )(fresh, q)
 
 
 def attend_kernel(
-    slots, places, info, pk, pv, fk, fv, q_ref, out_ref, stat_ref, keys, values, top, total, mixed, sem
+    slots, first, places, info, *refs
 ):
+    parts = refs[:PLANE]
+    fresh, q_ref, out_ref, stat_ref, keys, values, top, total, mixed, sem = refs[-10:]
     step = pl.program_id(0)
     prefix_rows = slots * PAGE_TOKENS
-    suffix_rows = fk.shape[0]
+    part_rows = fresh.shape[2]
+    suffix_rows = PLANE * part_rows
+    part_slots = slots // PLANE
+    entry = (first + step) * 8
 
     @pl.when(step == 0)
     def _():
         values[prefix_rows + suffix_rows :, :] = jnp.zeros((CHUNK, HEAD_SIZE), jnp.bfloat16)
-        moves = [
-            pltpu.make_async_copy(fk, keys.at[pl.ds(prefix_rows, suffix_rows), :], sem.at[2 * slots]),
-            pltpu.make_async_copy(
-                fv, values.at[pl.ds(prefix_rows, suffix_rows), :], sem.at[2 * slots + 1]
-            ),
-        ]
+        moves = []
+        for n in range(PLANE):
+            for which, whole in enumerate((keys, values)):
+                there = pl.ds(prefix_rows + n * part_rows, part_rows)
+                moves.append((fresh.at[n, which], whole.at[there, :]))
         for n in range(slots):
-            source = pl.ds(n * PAGE_TOKENS, PAGE_TOKENS)
+            source = pl.ds((n % part_slots) * PAGE_TOKENS, PAGE_TOKENS)
             there = pl.ds(pl.multiple_of(places[n] * PAGE_TOKENS, PAGE_TOKENS), PAGE_TOKENS)
-            moves.append(pltpu.make_async_copy(pk.at[source, :], keys.at[there, :], sem.at[n]))
-            moves.append(
-                pltpu.make_async_copy(pv.at[source, :], values.at[there, :], sem.at[slots + n])
-            )
+            for which, whole in enumerate((keys, values)):
+                moves.append((parts[n // part_slots].at[which, source, :], whole.at[there, :]))
+        moves = [pltpu.make_async_copy(*move, sem.at[n]) for n, move in enumerate(moves)]
         for move in moves:
             move.start()
         for move in moves:
@@ -223,9 +198,9 @@
     total[...] = jnp.zeros_like(total)
     mixed[...] = jnp.zeros_like(mixed)
     rows = q_ref.shape[1]
-    prefix_low, prefix_high = info[step * 8], info[step * 8 + 1]
-    suffix_low, suffix_high = info[step * 8 + 2], info[step * 8 + 3]
-    first_token = info[step * 8 + 4]
+    prefix_low, prefix_high = info[entry], info[entry + 1]
+    suffix_low, suffix_high = info[entry + 2], info[entry + 3]
+    first_token = info[entry + 4]
 
     def fold(offset, valid):
         offset = pl.multiple_of(offset, PAGE_TOKENS)
@@ -274,12 +249,12 @@
     stat_ref[0, 2:8, :] = jnp.zeros((6, rows), jnp.float32)
 
 
-def attend(places, info, pk, pv, fk, fv, queries):
-    pages, rows, _ = queries.shape
+def attend(places, info, parts, fresh, after, queries, first, pages):
+    _, rows, _ = queries.shape
     slots = places.shape[0]
-    span = pk.shape[0] + fk.shape[0] + CHUNK
+    span = (slots * PAGE_TOKENS) + PLANE * fresh.shape[2] + CHUNK
     return pl.pallas_call(
-        functools.partial(attend_kernel, slots),
+        functools.partial(attend_kernel, slots, first),
         out_shape=[
             jax.ShapeDtypeStruct((pages, HEAD_SIZE, rows), jnp.bfloat16),
             jax.ShapeDtypeStruct((pages, 8, rows), jnp.float32),
@@ -287,7 +262,8 @@
         grid_spec=pltpu.PrefetchScalarGridSpec(
             num_scalar_prefetch=2,
             grid=(pages,),
-            in_specs=[ANY] * 4 + [pl.BlockSpec((1, rows, HEAD_SIZE), lambda i, *_: (i, 0, 0))],
+            in_specs=[ANY] * (PLANE + 1 + len(after))
+            + [pl.BlockSpec((1, rows, HEAD_SIZE), lambda i, *_: (first + i, 0, 0))],
             out_specs=[
                 pl.BlockSpec((1, HEAD_SIZE, rows), lambda i, *_: (i, 0, 0)),
                 pl.BlockSpec((1, 8, rows), lambda i, *_: (i, 0, 0)),
@@ -298,66 +274,18 @@
                 pltpu.VMEM((1, rows), jnp.float32),
                 pltpu.VMEM((1, rows), jnp.float32),
                 pltpu.VMEM((HEAD_SIZE, rows), jnp.float32),
-                pltpu.SemaphoreType.DMA((2 * slots + 2,)),
+                pltpu.SemaphoreType.DMA((2 * slots + 2 * PLANE,)),
             ],
         ),
         compiler_params=pltpu.CompilerParams(vmem_limit_bytes=VMEM_LIMIT),
-    )(places, info, pk, pv, fk, fv, queries)
-
-
-def send_back_kernel(blocks, out, stat, out_all, stat_all, local_sem, send, recv):
-    me = lax.axis_index("page")
-    mine = lax.rem(me, PLANE)
-    block = lax.div(me, PLANE)
-    greet([lax.rem(block + d, blocks) * PLANE + mine for d in range(1, blocks)])
-    started = []
-    arriving = []
-    for d in range(1, blocks):
-        other = lax.rem(block + d, blocks)
-        for n, (source, whole) in enumerate(((out, out_all), (stat, stat_all))):
-            for slot, made in ((block, started), (lax.rem(block + blocks - d, blocks), arriving)):
-                made.append(
-                    pltpu.make_async_remote_copy(
-                        src_ref=source.at[other],
-                        dst_ref=whole.at[slot],
-                        send_sem=send.at[n, d - 1],
-                        recv_sem=recv.at[n, d - 1],
-                        device_id={"page": other * PLANE + mine},
-                        device_id_type=MESH,
-                    )
-                )
-            started[-1].start()
-    own = [
-        pltpu.make_async_copy(out.at[block], out_all.at[block], local_sem.at[0]),
-        pltpu.make_async_copy(stat.at[block], stat_all.at[block], local_sem.at[1]),
-    ]
-    for made in own:
-        made.start()
-    for made in arriving:
-        made.wait_recv()
-    for made in started:
-        made.wait_send()
-    for made in own:
-        made.wait()
-
-
-def send_back(out, stat):
-    blocks = out.shape[0]
-    return pl.pallas_call(
-        functools.partial(send_back_kernel, blocks),
-        out_shape=[
-            jax.ShapeDtypeStruct(out.shape, out.dtype),
-            jax.ShapeDtypeStruct(stat.shape, stat.dtype),
-        ],
-        in_specs=[ANY] * 2,
-        out_specs=[ANY] * 2,
-        scratch_shapes=[
-            pltpu.SemaphoreType.DMA((2,)),
-            pltpu.SemaphoreType.DMA((2, blocks - 1)),
-            pltpu.SemaphoreType.DMA((2, blocks - 1)),
-        ],
-        compiler_params=pltpu.CompilerParams(collective_id=1, has_side_effects=True),
-    )(out, stat)
+        cost_estimate=pl.CostEstimate(
+            flops=10**8, bytes_accessed=10**5, transcendentals=0
+        ),
+    )(places, info, *parts, *after, fresh, queries)
+
+
+def moved(block, axis_size, target):
+    return lax.ppermute(block, "page", [(p, target(p)) for p in range(axis_size)])
 
 
 def page_facts(pages, page_lengths, request_group):
@@ -431,7 +359,11 @@
     suffix_value_cache = place(fresh_value_rows)
 
     slots = PLANE * prefix_key_slots.shape[0] // PAGE_TOKENS
-    slot_ids = block * slots + jnp.arange(slots, dtype=jnp.int32)
+    part_slots = slots // PLANE
+    slot_parts = jnp.arange(slots, dtype=jnp.int32) // part_slots
+    slot_ids = (block * PLANE + (mine ^ slot_parts)) * part_slots + jnp.arange(
+        slots, dtype=jnp.int32
+    ) % part_slots
     map_group = jnp.arange(prefix_slot_map.shape[0], dtype=jnp.int32) // PREFIX_PAGES
     slot_group = jnp.sum(
         jnp.where(slot_ids[:, None] == prefix_slot_map[None, :], map_group[None, :], 0), axis=1
@@ -442,7 +374,8 @@
     )
     places = jnp.sum(ahead.astype(jnp.int32), axis=1)
     q_pages = (
-        (jnp.arange(blocks, dtype=jnp.int32) * PLANE + mine)[:, None] * pages_here
+        ((block + blocks - jnp.arange(blocks, dtype=jnp.int32)) % blocks * PLANE + mine)[:, None]
+        * pages_here
         + jnp.arange(pages_here, dtype=jnp.int32)
     ).reshape(-1)
     q_first, q_group = page_facts(q_pages, page_lengths, request_group)
@@ -462,21 +395,27 @@
 
     paged_queries = queries.reshape(pages_here, PAGE_TOKENS, heads, HEAD_SIZE).transpose(0, 2, 1, 3)
     paged_queries = paged_queries.reshape(pages_here * heads * PAGE_TOKENS, HEAD_SIZE)
-    pk, pv, fk, fv, q_all = gather(
-        prefix_key_slots, prefix_value_slots, fresh_key_rows, fresh_value_rows, paged_queries, blocks
-    )
-    out, stat = attend(
-        places,
-        info,
-        pk.reshape(-1, HEAD_SIZE),
-        pv.reshape(-1, HEAD_SIZE),
-        fk.reshape(-1, HEAD_SIZE),
-        fv.reshape(-1, HEAD_SIZE),
-        q_all.reshape(blocks * pages_here, heads * PAGE_TOKENS, HEAD_SIZE),
-    )
-    out, stat = send_back(
-        out.reshape(blocks, pages_here, HEAD_SIZE, -1), stat.reshape(blocks, pages_here, 8, -1)
-    )
+    size = lax.axis_size("page")
+    prefix = jnp.stack([prefix_key_slots, prefix_value_slots])
+    parts = (
+        prefix,
+        moved(prefix, size, lambda p: p ^ 1),
+        moved(prefix, size, lambda p: p ^ 2),
+        moved(prefix, size, lambda p: p ^ 3),
+    )
+    fresh, q_all = gather(jnp.stack([fresh_key_rows, fresh_value_rows]), paged_queries, blocks)
+    q_all = q_all.reshape(blocks * pages_here, heads * PAGE_TOKENS, HEAD_SIZE)
+    outs, stats = [], []
+    for d in [*range(1, blocks), 0]:
+        out, stat = attend(
+            places, info, parts, fresh, outs[-2:-1], q_all, d * pages_here, pages_here
+        )
+        if d:
+            back = lambda p, d=d: (p // PLANE + blocks - d) % blocks * PLANE + p % PLANE
+            out, stat = moved(out, size, back), moved(stat, size, back)
+        outs.append(out)
+        stats.append(stat)
+    out, stat = jnp.stack(outs), jnp.stack(stats)
     tops, totals = stat[:, :, 0, :], stat[:, :, 1, :]
     share = totals * jnp.exp(tops - jnp.max(tops, axis=0, keepdims=True))
     share = share / jnp.sum(share, axis=0, keepdims=True)

time: 183 us -> 176 us (0.962)
  the two profiles are of different devices: /device:TPU:13 before, /device:TPU:7 now
where the time goes in v1:
time: 176 us; the launch traced here: 177 us
  Pallas kernels  77.7 us (44%)
  starting transfers between devices  43.3 us (25%)
  other arithmetic  23.8 us (14%)
  local copies, waits for them, and re-layouts  14.1 us (8%)
  matrix products  13.9 us (8%)
  between operations  2.34 us (1%)
    pallas_call x1, Pallas kernels, gather(): pl.pallas_call(functools.partial(gather_kernel, blocks), out_shape=[jax.S...  38.9 us
    pallas_call x4, Pallas kernels, attend(): pl.pallas_call(functools.partial(attend_kernel, slots, first), out_shape=...  38.8 us
    ppermute x9, starting transfers between devices, moved(): lax.ppermute(block, 'page', [(p, target(p)) for p in range(axis_size)])  29.9 us
    ppermute x1, starting transfers between devices, local(): other_part = lax.ppermute(attn_part, 'kv', [(0, 1), (1, 0)])  13.3 us
    dot_general x1, matrix products, project(): jnp.dot(normed, w_query, preferred_element_type=jnp.float32)  4.4 us
    dot_general x1, matrix products, local(): jnp.dot(low_rank, laurel_right, preferred_element_type=jnp.float32)  3.74 us
    reduce_sum x3, other arithmetic, rms_scale(): jnp.mean(values * values, axis=-1, keepdims=True) + epsilon  3.66 us
  transfers between devices with their start and end apart: 10, of which 2 were waited for; matrix products, arithmetic and copies ran while one was open for 22% of the time, Pallas kernels for 39%

profile of v1, /device:TPU:7, one launch (start us, length us, event | category | flops | bytes accessed | tf_op | source)
XLA Modules:
  0.0 176.8 jit_solution(12952095764059026792)
XLA Ops:
  0.7 1.4 pad_maximum_fusion.refs_0_
  2.5 2.3 %collective-permute-start.2 = (bf16[2,1024,256]{2,1,0:T(8,128)(2,1)S(1)}, bf16[2,1024,256]{2,1,0:T(8,128)(2,1)}, u32[]{:S(2)}, u32[]{:S(2)}) collective-permute-start(bf16[2,1024,256]{2,1,0:T(8,128)(2,1)S(1)} %pad_maximum_fusion.refs_0_), channel_id=1, source_target_pairs={{0,3},{1,2},{2,1},{3,0},{4,7},{5,6},{6,5},{7,4},{8,11},{9,10},{10,... | collective-permute-start | bytes 3145736 | tf_op jit(solution)/shard_map/ppermute | solution.py:288
  6.2 1.5 fusion.2
  7.7 4.4 %fusion.34 = f32[256,1024]{1,0:T(8,128)} fusion(bf16[256,2048]{1,0:T(8,128)(2,1)S(1)} %fusion.2, bf16[2048,1024]{1,0:T(8,128)(2,1)} %param.20), kind=kOutput, calls=%fused_computation.111 | convolution fusion | flops 1073741824 | bytes 6291456 | tf_op jit(solution)/shard_map/dot_general | solution.py:61
  12.1 2.7 %reshape.469 = f32[256,4,256]{2,1,0:T(4,128)} reshape(f32[256,1024]{1,0:T(8,128)} %fusion.34) | data formatting | bytes 2097152 | tf_op jit(solution)/shard_map/reshape | solution.py:61
  14.8 1.6 multiply_reduce_fusion.3
  17.1 1.4 fusion.4
  22.6 1.7 multiply_reduce_fusion.4
  25.2 38.9 %shard_map.193 = (bf16[4,2,256,256]{3,2,1,0:T(8,128)(2,1)}, bf16[4,1024,256]{2,1,0:T(8,128)(2,1)}) custom-call(bf16[2,256,256]{2,1,0:T(8,128)(2,1)} %pad_maximum_fusion.1.fresh, bf16[1024,256]{1,0:T(8,128)(2,1)} %bitcast.86), custom_call_target="tpu_custom_call" | custom-call | flops 40000000000 | bytes 1000000 | tf_op jit(solution)/shard_map/pallas_call | solution.py:146
  65.0 1.4 select_reduce_fusion.1
  72.1 1.4 stack.56
  76.1 8.9 %shard_map.194 = (bf16[2,256,512]{2,1,0:T(8,128)(2,1)}, f32[2,8,512]{2,1,0:T(8,128)}) custom-call(s32[32]{0:T(128)} %convert_reduce_fusion.places, s32[64]{0:T(128)} %reshape.468.info, bf16[2,1024,256]{2,1,0:T(8,128)(2,1)} %copy-done.1, bf16[2,1024,256]{2,1,0:T(8,128)(2,1)} %collective-permute-done.refs_1_, ...), custom_call_target="tpu_custom_call" | custom-call | flops 100000000 | bytes 100000 | tf_op jit(solution)/shard_map/pallas_call | solution.py:256
  85.0 13.0 %collective-permute-start.3 = (bf16[2,256,512]{2,1,0:T(8,128)(2,1)}, bf16[2,256,512]{2,1,0:T(8,128)(2,1)S(1)}, u32[]{:S(2)}, u32[]{:S(2)}) collective-permute-start(bf16[2,256,512]{2,1,0:T(8,128)(2,1)} %get-tuple-element.15), channel_id=1, source_target_pairs={{0,12},{1,13},{2,14},{3,15},{4,0},{5,1},{6,2},{7,3},{8,4},{9,5},{1... | collective-permute-start | bytes 1572872 | tf_op jit(solution)/shard_map/ppermute | solution.py:288
  98.0 8.9 %shard_map.195 = (bf16[2,256,512]{2,1,0:T(8,128)(2,1)}, f32[2,8,512]{2,1,0:T(8,128)}) custom-call(s32[32]{0:T(128)} %convert_reduce_fusion.places, s32[64]{0:T(128)} %reshape.468.info, bf16[2,1024,256]{2,1,0:T(8,128)(2,1)} %copy-done.1, bf16[2,1024,256]{2,1,0:T(8,128)(2,1)} %collective-permute-done.refs_1_, ...), custom_call_target="tpu_custom_call" | custom-call | flops 100000000 | bytes 100000 | tf_op jit(solution)/shard_map/pallas_call | solution.py:256
  106.8 1.4 collective-permute-start.4
  111.0 8.9 %shard_map.196 = (bf16[2,256,512]{2,1,0:T(8,128)(2,1)}, f32[2,8,512]{2,1,0:T(8,128)}) custom-call(s32[32]{0:T(128)} %convert_reduce_fusion.places, s32[64]{0:T(128)} %reshape.468.info, bf16[2,1024,256]{2,1,0:T(8,128)(2,1)} %copy-done.1, bf16[2,1024,256]{2,1,0:T(8,128)(2,1)} %collective-permute-done.refs_1_, ...), custom_call_target="tpu_custom_call" | custom-call | flops 100000000 | bytes 100000 | tf_op jit(solution)/shard_map/pallas_call | solution.py:256
  119.9 10.8 %collective-permute-start.8 = (f32[2,8,512]{2,1,0:T(8,128)}, f32[2,8,512]{2,1,0:T(8,128)S(1)}, u32[]{:S(2)}, u32[]{:S(2)}) collective-permute-start(f32[2,8,512]{2,1,0:T(8,128)} %get-tuple-element.21), channel_id=1, source_target_pairs={{0,4},{1,5},{2,6},{3,7},{4,8},{5,9},{6,10},{7,11},{8,12},{9,13},{1... | collective-permute-start | bytes 98312 | tf_op jit(solution)/shard_map/ppermute | solution.py:288
  133.6 1.4 collective-permute-done.4.refs_4_
  135.7 12.2 %shard_map.197 = (bf16[2,256,512]{2,1,0:T(8,128)(2,1)}, f32[2,8,512]{2,1,0:T(8,128)}) custom-call(s32[32]{0:T(128)} %convert_reduce_fusion.places, s32[64]{0:T(128)} %reshape.468.info, bf16[2,1024,256]{2,1,0:T(8,128)(2,1)} %copy-done.1, bf16[2,1024,256]{2,1,0:T(8,128)(2,1)} %collective-permute-done.refs_1_, ...), custom_call_target="tpu_custom_call" | custom-call | flops 100000000 | bytes 100000 | tf_op jit(solution)/shard_map/pallas_call | solution.py:256
  148.9 1.6 multiply_reduce_fusion
  151.3 3.5 %convolution_convert_fusion = bf16[256,2048]{1,0:T(8,128)(2,1)S(1)} fusion(bf16[256,1024]{1,0:T(8,128)(2,1)S(1)} %bitcast.87, bf16[1024,2048]{1,0:T(8,128)(2,1)} %param.25), kind=kOutput, calls=%fused_computation.3 | convolution fusion | flops 1074266112 | bytes 5767168 | tf_op jit(solution)/shard_map/dot_general | solution.py:428
  154.8 13.3 %collective-permute-start.9 = (bf16[256,2048]{1,0:T(8,128)(2,1)S(1)}, bf16[256,2048]{1,0:T(8,128)(2,1)}, u32[]{:S(2)}, u32[]{:S(2)}) collective-permute-start(bf16[256,2048]{1,0:T(8,128)(2,1)S(1)} %convolution_convert_fusion), channel_id=1, source_target_pairs={{0,16},{16,0},{1,17},{17,1},{2,18},{18,2},{3,19},{19,3},{4,20},{20... | collective-permute-start | bytes 3145736 | tf_op jit(solution)/shard_map/ppermute | solution.py:429
  169.5 3.7 %multiply_reduce_fusion.1 = (f32[256]{0:T(256)S(1)}, f32[256,2048]{1,0:T(8,128)}) fusion(bf16[64,2048]{1,0:T(8,128)(2,1)} %param.28, bf16[256,2048]{1,0:T(8,128)(2,1)S(1)} %fusion.2, bf16[2048,64]{0,1:T(8,128)(2,1)} %param.27), kind=kOutput, calls=%fused_computation.7 | convolution fusion | flops 135282432 | bytes 3671040 | tf_op jit(solution)/shard_map/dot_general | solution.py:438
  173.3 1.8 %multiply_reduce_fusion.2 = (f32[256]{0:T(256)S(1)}, f32[256,2048]{1,0:T(8,128)S(1)}) fusion(bf16[256,2048]{1,0:T(8,128)(2,1)} %collective-permute-done.9, bf16[256,2048]{1,0:T(8,128)(2,1)S(1)} %convolution_convert_fusion), kind=kLoop, calls=%fused_computation.8 | loop fusion | flops 2621184 | bytes 4195328 | tf_op jit(solution)/shard_map/reduce_sum | solution.py:31
  (116 shorter events, 26.2 us)
Async XLA Ops:
  0.6 18.9 %copy-start = (bf16[2048,256]{1,0:T(8,128)(2,1)S(1)}, bf16[2048,256]{1,0:T(8,128)(2,1)}, u32[]{:S(2)}) copy-start(bf16[2048,256]{1,0:T(8,128)(2,1)} %param.21) | copy-start | bytes 3145732
  0.6 4.2 %copy-start.20 = (s32[8]{0:T(128)S(1)}, s32[8]{0:T(128)}, u32[]{:S(2)}) copy-start(s32[8]{0:T(128)} %param.33) | copy-start | bytes 100
  0.7 4.6 %copy-start.17 = (s32[2]{0:T(128)S(1)}, s32[2]{0:T(128)}, u32[]{:S(2)}) copy-start(s32[2]{0:T(128)} %param.35) | copy-start | bytes 28
  0.7 5.2 %copy-start.2 = (bf16[256,2048]{1,0:T(8,128)(2,1)S(1)}, bf16[256,2048]{1,0:T(8,128)(2,1)}, u32[]{:S(2)}) copy-start(bf16[256,2048]{1,0:T(8,128)(2,1)} %param.18) | copy-start | bytes 3145732
  0.7 5.5 %copy-start.11 = (f32[2048]{0:T(1024)S(1)}, f32[2048]{0:T(1024)}, u32[]{:S(2)}) copy-start(f32[2048]{0:T(1024)} %param.19) | copy-start | bytes 24580
  2.1 10.0 %copy-start.1 = (bf16[2,1024,256]{2,1,0:T(8,128)(2,1)}, bf16[2,1024,256]{2,1,0:T(8,128)(2,1)S(1)}, u32[]{:S(2)}) copy-start(bf16[2,1024,256]{2,1,0:T(8,128)(2,1)S(1)} %pad_maximum_fusion.refs_0_) | copy-start | bytes 3145732
  2.1 73.9 %collective-permute-start = (bf16[2,1024,256]{2,1,0:T(8,128)(2,1)S(1)}, bf16[2,1024,256]{2,1,0:T(8,128)(2,1)}, u32[]{:S(2)}, u32[]{:S(2)}) collective-permute-start(bf16[2,1024,256]{2,1,0:T(8,128)(2,1)S(1)} %pad_maximum_fusion.refs_0_), channel_id=1, source_target_pairs={{0,1},{1,0},{2,3},{3,2},{4,5},{5,4},{6,7},{7,6},{8,9},{9,8},{10,11... | collective-permute-start | bytes 3145736 | tf_op jit(solution)/shard_map/ppermute | solution.py:288
  2.5 73.6 %collective-permute-start.1 = (bf16[2,1024,256]{2,1,0:T(8,128)(2,1)S(1)}, bf16[2,1024,256]{2,1,0:T(8,128)(2,1)}, u32[]{:S(2)}, u32[]{:S(2)}) collective-permute-start(bf16[2,1024,256]{2,1,0:T(8,128)(2,1)S(1)} %pad_maximum_fusion.refs_0_), channel_id=1, source_target_pairs={{0,2},{1,3},{2,0},{3,1},{4,6},{5,7},{6,4},{7,5},{8,10},{9,11},{10,... | collective-permute-start | bytes 3145736 | tf_op jit(solution)/shard_map/ppermute | solution.py:288
  2.5 73.5 %collective-permute-start.2 = (bf16[2,1024,256]{2,1,0:T(8,128)(2,1)S(1)}, bf16[2,1024,256]{2,1,0:T(8,128)(2,1)}, u32[]{:S(2)}, u32[]{:S(2)}) collective-permute-start(bf16[2,1024,256]{2,1,0:T(8,128)(2,1)S(1)} %pad_maximum_fusion.refs_0_), channel_id=1, source_target_pairs={{0,3},{1,2},{2,1},{3,0},{4,7},{5,6},{6,5},{7,4},{8,11},{9,10},{10,... | collective-permute-start | bytes 3145736 | tf_op jit(solution)/shard_map/ppermute | solution.py:288
  5.0 7.1 %copy-start.13 = (s32[8]{0:T(128)}, s32[8]{0:T(128)S(1)}, u32[]{:S(2)}) copy-start(s32[8]{0:T(128)S(1)} %add.246) | copy-start | bytes 100
  12.1 4.9 %copy-start.15 = (f32[256]{0:T(256)S(1)}, f32[256]{0:T(256)}, u32[]{:S(2)}) copy-start(f32[256]{0:T(256)} %param.23) | copy-start | bytes 3076
  24.3 39.8 %copy-start.9 = (f32[256]{0:T(256)}, f32[256]{0:T(256)S(1)}, u32[]{:S(2)}) copy-start(f32[256]{0:T(256)S(1)} %add_rsqrt_fusion.3) | copy-start | bytes 3076
  84.9 23.3 %copy-start.19 = (f32[2,8,512]{2,1,0:T(8,128)S(1)}, f32[2,8,512]{2,1,0:T(8,128)}, u32[]{:S(2)}) copy-start(f32[2,8,512]{2,1,0:T(8,128)} %get-tuple-element.19) | copy-start | bytes 98308
  85.0 25.2 %collective-permute-start.3 = (bf16[2,256,512]{2,1,0:T(8,128)(2,1)}, bf16[2,256,512]{2,1,0:T(8,128)(2,1)S(1)}, u32[]{:S(2)}, u32[]{:S(2)}) collective-permute-start(bf16[2,256,512]{2,1,0:T(8,128)(2,1)} %get-tuple-element.15), channel_id=1, source_target_pairs={{0,12},{1,13},{2,14},{3,15},{4,0},{5,1},{6,2},{7,3},{8,4},{9,5},{1... | collective-permute-start | bytes 1572872 | tf_op jit(solution)/shard_map/ppermute | solution.py:288
  106.8 28.1 %collective-permute-start.4 = (bf16[2,256,512]{2,1,0:T(8,128)(2,1)}, bf16[2,256,512]{2,1,0:T(8,128)(2,1)S(1)}, u32[]{:S(2)}, u32[]{:S(2)}) collective-permute-start(bf16[2,256,512]{2,1,0:T(8,128)(2,1)} %get-tuple-element.16), channel_id=1, source_target_pairs={{0,8},{1,9},{2,10},{3,11},{4,12},{5,13},{6,14},{7,15},{8,0},{9,1},... | collective-permute-start | bytes 1572872 | tf_op jit(solution)/shard_map/ppermute | solution.py:288
  108.3 39.7 %collective-permute-start.6 = (f32[2,8,512]{2,1,0:T(8,128)S(1)}, f32[2,8,512]{2,1,0:T(8,128)S(1)}, u32[]{:S(2)}, u32[]{:S(2)}) collective-permute-start(f32[2,8,512]{2,1,0:T(8,128)S(1)} %copy-done.19), channel_id=1, source_target_pairs={{0,12},{1,13},{2,14},{3,15},{4,0},{5,1},{6,2},{7,3},{8,4},{9,5},{1... | collective-permute-start | bytes 98312 | tf_op jit(solution)/shard_map/ppermute | solution.py:288
  109.2 21.7 %copy-start.10 = (f32[256]{0:T(256)S(1)}, f32[256]{0:T(256)}, u32[]{:S(2)}) copy-start(f32[256]{0:T(256)} %copy-done.9) | copy-start | bytes 3076
  109.2 22.5 %copy-start.18 = (s32[2]{0:T(128)S(1)}, s32[2]{0:T(128)}, u32[]{:S(2)}) copy-start(s32[2]{0:T(128)} %get-tuple-element.54) | copy-start | bytes 28
  109.2 38.8 %collective-permute-start.7 = (f32[2,8,512]{2,1,0:T(8,128)}, f32[2,8,512]{2,1,0:T(8,128)S(1)}, u32[]{:S(2)}, u32[]{:S(2)}) collective-permute-start(f32[2,8,512]{2,1,0:T(8,128)} %get-tuple-element.20), channel_id=1, source_target_pairs={{0,8},{1,9},{2,10},{3,11},{4,12},{5,13},{6,14},{7,15},{8,0},{9,1},... | collective-permute-start | bytes 98312 | tf_op jit(solution)/shard_map/ppermute | solution.py:288
  119.9 28.1 %collective-permute-start.8 = (f32[2,8,512]{2,1,0:T(8,128)}, f32[2,8,512]{2,1,0:T(8,128)S(1)}, u32[]{:S(2)}, u32[]{:S(2)}) collective-permute-start(f32[2,8,512]{2,1,0:T(8,128)} %get-tuple-element.21), channel_id=1, source_target_pairs={{0,4},{1,5},{2,6},{3,7},{4,8},{5,9},{6,10},{7,11},{8,12},{9,13},{1... | collective-permute-start | bytes 98312 | tf_op jit(solution)/shard_map/ppermute | solution.py:288
  130.7 18.2 %collective-permute-start.5 = (bf16[2,256,512]{2,1,0:T(8,128)(2,1)}, bf16[2,256,512]{2,1,0:T(8,128)(2,1)S(1)}, u32[]{:S(2)}, u32[]{:S(2)}) collective-permute-start(bf16[2,256,512]{2,1,0:T(8,128)(2,1)} %get-tuple-element.17), channel_id=1, source_target_pairs={{0,4},{1,5},{2,6},{3,7},{4,8},{5,9},{6,10},{7,11},{8,12},{9,13},{1... | collective-permute-start | bytes 1572872 | tf_op jit(solution)/shard_map/ppermute | solution.py:288
  133.6 15.4 %copy-start.6 = (bf16[2,256,512]{2,1,0:T(8,128)(2,1)S(1)}, bf16[2,256,512]{2,1,0:T(8,128)(2,1)}, u32[]{:S(2)}) copy-start(bf16[2,256,512]{2,1,0:T(8,128)(2,1)} %copy-done.5) | copy-start | bytes 1572868
  151.3 17.6 %copy-start.8 = (bf16[256,256]{1,0:T(8,128)(2,1)S(1)}, bf16[256,256]{1,0:T(8,128)(2,1)}, u32[]{:S(2)}) copy-start(bf16[256,256]{1,0:T(8,128)(2,1)} %multiply_convert_fusion.1) | copy-start | bytes 393220
  154.8 18.5 %collective-permute-start.9 = (bf16[256,2048]{1,0:T(8,128)(2,1)S(1)}, bf16[256,2048]{1,0:T(8,128)(2,1)}, u32[]{:S(2)}, u32[]{:S(2)}) collective-permute-start(bf16[256,2048]{1,0:T(8,128)(2,1)S(1)} %convolution_convert_fusion), channel_id=1, source_target_pairs={{0,16},{16,0},{1,17},{17,1},{2,18},{18,2},{3,19},{19,3},{4,20},{20... | collective-permute-start | bytes 3145736 | tf_op jit(solution)/shard_map/ppermute | solution.py:429
  (9 other events, 14.5 us)

commit v2 on v1

--- a/solution.py
+++ b/solution.py
@@ -408,7 +408,7 @@
     outs, stats = [], []
     for d in [*range(1, blocks), 0]:
         out, stat = attend(
-            places, info, parts, fresh, outs[-2:-1], q_all, d * pages_here, pages_here
+            places, info, parts, fresh, outs[-2:-1] if d else [], q_all, d * pages_here, pages_here
         )
         if d:
             back = lambda p, d=d: (p // PLANE + blocks - d) % blocks * PLANE + p % PLANE

time: 176 us -> 164 us (0.932); the launches traced: 177 us -> 163 us
  starting transfers between devices: 43.3 us -> 17.4 us
  Pallas kernels: 77.7 us -> 84.4 us
  waiting for transfers between devices: 1.56 us -> 7.88 us
    ppermute x9, starting transfers between devices: 29.9 us -> 15.9 us  [moved(): lax.ppermute(block, 'page', [(p, target(p)) for p in range(axis_size)])]
    ppermute x1, starting transfers between devices: 13.3 us -> 1.51 us  [local(): other_part = lax.ppermute(attn_part, 'kv', [(0, 1), (1, 0)])]
    pallas_call x4, Pallas kernels: 38.8 us -> 45.5 us  [attend(): pl.pallas_call(functools.partial(attend_kernel, slots, first), out_shape=...]
    ppermute x9, waiting for transfers between devices: 1.56 us -> 7.88 us  [moved(): lax.ppermute(block, 'page', [(p, target(p)) for p in range(axis_size)])]
  transfers between devices with their start and end apart: 10 -> 10, of which waited for: 2 -> 1; matrix products, arithmetic and copies ran while one was open for 22% -> 24% of each run, Pallas kernels for 39% -> 45%
where the time goes in v2:
time: 164 us; the launch traced here: 163 us
  Pallas kernels  84.4 us (51%)
  other arithmetic  23.7 us (14%)
  starting transfers between devices  17.4 us (11%)
  matrix products  13.9 us (8%)
  local copies, waits for them, and re-layouts  13.3 us (8%)
  waiting for transfers between devices  7.88 us (5%)
  between operations  2.36 us (1%)
    pallas_call x4, Pallas kernels, attend(): pl.pallas_call(functools.partial(attend_kernel, slots, first), out_shape=...  45.5 us
    pallas_call x1, Pallas kernels, gather(): pl.pallas_call(functools.partial(gather_kernel, blocks), out_shape=[jax.S...  38.9 us
    ppermute x9, starting transfers between devices, moved(): lax.ppermute(block, 'page', [(p, target(p)) for p in range(axis_size)])  15.9 us
    ppermute x9, waiting for transfers between devices, moved(): lax.ppermute(block, 'page', [(p, target(p)) for p in range(axis_size)])  7.88 us
    dot_general x1, matrix products, project(): jnp.dot(normed, w_query, preferred_element_type=jnp.float32)  4.41 us
    dot_general x1, matrix products, local(): jnp.dot(low_rank, laurel_right, preferred_element_type=jnp.float32)  3.74 us
    reduce_sum x3, other arithmetic, rms_scale(): jnp.mean(values * values, axis=-1, keepdims=True) + epsilon  3.66 us
    dot_general x1, matrix products, local(): jnp.dot(attended, w_out, preferred_element_type=jnp.float32)  3.5 us
  transfers between devices with their start and end apart: 10, of which 1 were waited for; matrix products, arithmetic and copies ran while one was open for 24% of the time, Pallas kernels for 45%

profile of v2, /device:TPU:7, one launch (start us, length us, event | category | flops | bytes accessed | tf_op | source)
XLA Modules:
  0.0 163.0 jit_solution(2739864697964218636)
XLA Ops:
  0.7 1.4 pad_maximum_fusion.refs_0_
  2.5 2.3 %collective-permute-start.2 = (bf16[2,1024,256]{2,1,0:T(8,128)(2,1)S(1)}, bf16[2,1024,256]{2,1,0:T(8,128)(2,1)}, u32[]{:S(2)}, u32[]{:S(2)}) collective-permute-start(bf16[2,1024,256]{2,1,0:T(8,128)(2,1)S(1)} %pad_maximum_fusion.refs_0_), channel_id=1, source_target_pairs={{0,3},{1,2},{2,1},{3,0},{4,7},{5,6},{6,5},{7,4},{8,11},{9,10},{10,... | collective-permute-start | bytes 3145736 | tf_op jit(solution)/shard_map/ppermute | solution.py:288
  6.1 1.5 fusion.2
  7.6 4.4 %fusion.34 = f32[256,1024]{1,0:T(8,128)} fusion(bf16[256,2048]{1,0:T(8,128)(2,1)S(1)} %fusion.2, bf16[2048,1024]{1,0:T(8,128)(2,1)} %param.20), kind=kOutput, calls=%fused_computation.111 | convolution fusion | flops 1073741824 | bytes 6291456 | tf_op jit(solution)/shard_map/dot_general | solution.py:61
  12.1 2.7 %reshape.469 = f32[256,4,256]{2,1,0:T(4,128)} reshape(f32[256,1024]{1,0:T(8,128)} %fusion.34) | data formatting | bytes 2097152 | tf_op jit(solution)/shard_map/reshape | solution.py:61
  14.8 1.6 multiply_reduce_fusion.3
  17.0 1.4 fusion.4
  22.5 1.7 %multiply_reduce_fusion.4 = (f32[256]{0:T(256)S(1)}, f32[256,256]{1,0:T(8,128)S(1)}) fusion(bf16[256,2048]{1,0:T(8,128)(2,1)S(1)} %fusion.2, bf16[2048,256]{1,0:T(8,128)(2,1)} %param.22), kind=kOutput, calls=%fused_computation.22 | convolution fusion | flops 268566272 | bytes 2360320 | tf_op jit(solution)/shard_map/dot_general | solution.py:71
  25.1 38.9 %shard_map.193 = (bf16[4,2,256,256]{3,2,1,0:T(8,128)(2,1)}, bf16[4,1024,256]{2,1,0:T(8,128)(2,1)}) custom-call(bf16[2,256,256]{2,1,0:T(8,128)(2,1)} %pad_maximum_fusion.1.fresh, bf16[1024,256]{1,0:T(8,128)(2,1)} %bitcast.86), custom_call_target="tpu_custom_call" | custom-call | flops 40000000000 | bytes 1000000 | tf_op jit(solution)/shard_map/pallas_call | solution.py:146
  64.9 1.4 select_reduce_fusion.1
  72.0 1.4 stack.56
  74.6 1.5 convert_reduce_fusion.places
  76.1 10.5 %shard_map.194 = (bf16[2,256,512]{2,1,0:T(8,128)(2,1)}, f32[2,8,512]{2,1,0:T(8,128)}) custom-call(s32[32]{0:T(128)} %convert_reduce_fusion.places, s32[64]{0:T(128)} %reshape.468.info, bf16[2,1024,256]{2,1,0:T(8,128)(2,1)} %copy-done.1, bf16[2,1024,256]{2,1,0:T(8,128)(2,1)} %collective-permute-done.refs_1_, ...), custom_call_target="tpu_custom_call" | custom-call | flops 100000000 | bytes 100000 | tf_op jit(solution)/shard_map/pallas_call | solution.py:256
  86.6 9.8 %collective-permute-start.3 = (bf16[2,256,512]{2,1,0:T(8,128)(2,1)}, bf16[2,256,512]{2,1,0:T(8,128)(2,1)S(1)}, u32[]{:S(2)}, u32[]{:S(2)}) collective-permute-start(bf16[2,256,512]{2,1,0:T(8,128)(2,1)} %get-tuple-element.15), channel_id=1, source_target_pairs={{0,12},{1,13},{2,14},{3,15},{4,0},{5,1},{6,2},{7,3},{8,4},{9,5},{1... | collective-permute-start | bytes 1572872 | tf_op jit(solution)/shard_map/ppermute | solution.py:288
  96.4 10.5 %shard_map.195 = (bf16[2,256,512]{2,1,0:T(8,128)(2,1)}, f32[2,8,512]{2,1,0:T(8,128)}) custom-call(s32[32]{0:T(128)} %convert_reduce_fusion.places, s32[64]{0:T(128)} %reshape.468.info, bf16[2,1024,256]{2,1,0:T(8,128)(2,1)} %copy-done.1, bf16[2,1024,256]{2,1,0:T(8,128)(2,1)} %collective-permute-done.refs_1_, ...), custom_call_target="tpu_custom_call" | custom-call | flops 100000000 | bytes 100000 | tf_op jit(solution)/shard_map/pallas_call | solution.py:256
  106.9 1.4 collective-permute-start.7
  110.2 10.5 %shard_map.196 = (bf16[2,256,512]{2,1,0:T(8,128)(2,1)}, f32[2,8,512]{2,1,0:T(8,128)}) custom-call(s32[32]{0:T(128)} %convert_reduce_fusion.places, s32[64]{0:T(128)} %reshape.468.info, bf16[2,1024,256]{2,1,0:T(8,128)(2,1)} %copy-done.1, bf16[2,1024,256]{2,1,0:T(8,128)(2,1)} %collective-permute-done.refs_1_, ...), custom_call_target="tpu_custom_call" | custom-call | flops 100000000 | bytes 100000 | tf_op jit(solution)/shard_map/pallas_call | solution.py:256
  124.3 14.0 %shard_map.197 = (bf16[2,256,512]{2,1,0:T(8,128)(2,1)}, f32[2,8,512]{2,1,0:T(8,128)}) custom-call(s32[32]{0:T(128)} %convert_reduce_fusion.places, s32[64]{0:T(128)} %reshape.468.info, bf16[2,1024,256]{2,1,0:T(8,128)(2,1)} %copy-done.1, bf16[2,1024,256]{2,1,0:T(8,128)(2,1)} %collective-permute-done.refs_1_, ...), custom_call_target="tpu_custom_call" | custom-call | flops 100000000 | bytes 100000 | tf_op jit(solution)/shard_map/pallas_call | solution.py:256
  139.3 7.9 %collective-permute-done.4 = bf16[2,256,512]{2,1,0:T(8,128)(2,1)S(1)} collective-permute-done((bf16[2,256,512]{2,1,0:T(8,128)(2,1)}, bf16[2,256,512]{2,1,0:T(8,128)(2,1)S(1)}, u32[]{:S(2)}, u32[]{:S(2)}) %collective-permute-start.4) | collective-permute-done | bytes 524320 | tf_op jit(solution)/shard_map/ppermute | solution.py:288
  147.1 1.5 multiply_reduce_fusion
  149.4 3.5 %convolution_convert_fusion = bf16[256,2048]{1,0:T(8,128)(2,1)S(1)} fusion(bf16[256,1024]{1,0:T(8,128)(2,1)S(1)} %bitcast.87, bf16[1024,2048]{1,0:T(8,128)(2,1)} %param.25), kind=kOutput, calls=%fused_computation.3 | convolution fusion | flops 1074266112 | bytes 5767168 | tf_op jit(solution)/shard_map/dot_general | solution.py:428
  152.9 1.5 collective-permute-start.9
  155.8 3.7 %multiply_reduce_fusion.1 = (f32[256]{0:T(256)S(1)}, f32[256,2048]{1,0:T(8,128)}) fusion(bf16[64,2048]{1,0:T(8,128)(2,1)} %param.28, bf16[256,2048]{1,0:T(8,128)(2,1)S(1)} %fusion.2, bf16[2048,64]{0,1:T(8,128)(2,1)} %param.27), kind=kOutput, calls=%fused_computation.7 | convolution fusion | flops 135282432 | bytes 3671040 | tf_op jit(solution)/shard_map/dot_general | solution.py:438
  159.6 1.8 %multiply_reduce_fusion.2 = (f32[256]{0:T(256)S(1)}, f32[256,2048]{1,0:T(8,128)S(1)}) fusion(bf16[256,2048]{1,0:T(8,128)(2,1)} %collective-permute-done.9, bf16[256,2048]{1,0:T(8,128)(2,1)S(1)} %convolution_convert_fusion), kind=kLoop, calls=%fused_computation.8 | loop fusion | flops 2621184 | bytes 4195328 | tf_op jit(solution)/shard_map/reduce_sum | solution.py:31
  (114 shorter events, 23.7 us)
Async XLA Ops:
  0.6 18.9 %copy-start = (bf16[2048,256]{1,0:T(8,128)(2,1)S(1)}, bf16[2048,256]{1,0:T(8,128)(2,1)}, u32[]{:S(2)}) copy-start(bf16[2048,256]{1,0:T(8,128)(2,1)} %param.21) | copy-start | bytes 3145732
  0.6 4.2 %copy-start.19 = (s32[8]{0:T(128)S(1)}, s32[8]{0:T(128)}, u32[]{:S(2)}) copy-start(s32[8]{0:T(128)} %param.33) | copy-start | bytes 100
  0.7 4.6 %copy-start.16 = (s32[2]{0:T(128)S(1)}, s32[2]{0:T(128)}, u32[]{:S(2)}) copy-start(s32[2]{0:T(128)} %param.35) | copy-start | bytes 28
  0.7 5.1 %copy-start.2 = (bf16[256,2048]{1,0:T(8,128)(2,1)S(1)}, bf16[256,2048]{1,0:T(8,128)(2,1)}, u32[]{:S(2)}) copy-start(bf16[256,2048]{1,0:T(8,128)(2,1)} %param.18) | copy-start | bytes 3145732
  0.7 5.4 %copy-start.10 = (f32[2048]{0:T(1024)S(1)}, f32[2048]{0:T(1024)}, u32[]{:S(2)}) copy-start(f32[2048]{0:T(1024)} %param.19) | copy-start | bytes 24580
  2.1 9.9 %copy-start.1 = (bf16[2,1024,256]{2,1,0:T(8,128)(2,1)}, bf16[2,1024,256]{2,1,0:T(8,128)(2,1)S(1)}, u32[]{:S(2)}) copy-start(bf16[2,1024,256]{2,1,0:T(8,128)(2,1)S(1)} %pad_maximum_fusion.refs_0_) | copy-start | bytes 3145732
  2.1 74.0 %collective-permute-start = (bf16[2,1024,256]{2,1,0:T(8,128)(2,1)S(1)}, bf16[2,1024,256]{2,1,0:T(8,128)(2,1)}, u32[]{:S(2)}, u32[]{:S(2)}) collective-permute-start(bf16[2,1024,256]{2,1,0:T(8,128)(2,1)S(1)} %pad_maximum_fusion.refs_0_), channel_id=1, source_target_pairs={{0,1},{1,0},{2,3},{3,2},{4,5},{5,4},{6,7},{7,6},{8,9},{9,8},{10,11... | collective-permute-start | bytes 3145736 | tf_op jit(solution)/shard_map/ppermute | solution.py:288
  2.5 73.6 %collective-permute-start.1 = (bf16[2,1024,256]{2,1,0:T(8,128)(2,1)S(1)}, bf16[2,1024,256]{2,1,0:T(8,128)(2,1)}, u32[]{:S(2)}, u32[]{:S(2)}) collective-permute-start(bf16[2,1024,256]{2,1,0:T(8,128)(2,1)S(1)} %pad_maximum_fusion.refs_0_), channel_id=1, source_target_pairs={{0,2},{1,3},{2,0},{3,1},{4,6},{5,7},{6,4},{7,5},{8,10},{9,11},{10,... | collective-permute-start | bytes 3145736 | tf_op jit(solution)/shard_map/ppermute | solution.py:288
  2.5 73.6 %collective-permute-start.2 = (bf16[2,1024,256]{2,1,0:T(8,128)(2,1)S(1)}, bf16[2,1024,256]{2,1,0:T(8,128)(2,1)}, u32[]{:S(2)}, u32[]{:S(2)}) collective-permute-start(bf16[2,1024,256]{2,1,0:T(8,128)(2,1)S(1)} %pad_maximum_fusion.refs_0_), channel_id=1, source_target_pairs={{0,3},{1,2},{2,1},{3,0},{4,7},{5,6},{6,5},{7,4},{8,11},{9,10},{10,... | collective-permute-start | bytes 3145736 | tf_op jit(solution)/shard_map/ppermute | solution.py:288
  5.0 7.1 %copy-start.12 = (s32[8]{0:T(128)}, s32[8]{0:T(128)S(1)}, u32[]{:S(2)}) copy-start(s32[8]{0:T(128)S(1)} %add.246) | copy-start | bytes 100
  12.1 4.9 %copy-start.14 = (f32[256]{0:T(256)S(1)}, f32[256]{0:T(256)}, u32[]{:S(2)}) copy-start(f32[256]{0:T(256)} %param.23) | copy-start | bytes 3076
  24.3 39.8 %copy-start.8 = (f32[256]{0:T(256)}, f32[256]{0:T(256)S(1)}, u32[]{:S(2)}) copy-start(f32[256]{0:T(256)S(1)} %add_rsqrt_fusion.3) | copy-start | bytes 3076
  86.6 21.7 %copy-start.18 = (f32[2,8,512]{2,1,0:T(8,128)S(1)}, f32[2,8,512]{2,1,0:T(8,128)}, u32[]{:S(2)}) copy-start(f32[2,8,512]{2,1,0:T(8,128)} %get-tuple-element.19) | copy-start | bytes 98308
  86.6 22.8 %collective-permute-start.3 = (bf16[2,256,512]{2,1,0:T(8,128)(2,1)}, bf16[2,256,512]{2,1,0:T(8,128)(2,1)S(1)}, u32[]{:S(2)}, u32[]{:S(2)}) collective-permute-start(bf16[2,256,512]{2,1,0:T(8,128)(2,1)} %get-tuple-element.15), channel_id=1, source_target_pairs={{0,12},{1,13},{2,14},{3,15},{4,0},{5,1},{6,2},{7,3},{8,4},{9,5},{1... | collective-permute-start | bytes 1572872 | tf_op jit(solution)/shard_map/ppermute | solution.py:288
  106.9 31.4 %collective-permute-start.7 = (f32[2,8,512]{2,1,0:T(8,128)}, f32[2,8,512]{2,1,0:T(8,128)S(1)}, u32[]{:S(2)}, u32[]{:S(2)}) collective-permute-start(f32[2,8,512]{2,1,0:T(8,128)} %get-tuple-element.20), channel_id=1, source_target_pairs={{0,8},{1,9},{2,10},{3,11},{4,12},{5,13},{6,14},{7,15},{8,0},{9,1},... | collective-permute-start | bytes 98312 | tf_op jit(solution)/shard_map/ppermute | solution.py:288
  108.3 30.0 %collective-permute-start.6 = (f32[2,8,512]{2,1,0:T(8,128)S(1)}, f32[2,8,512]{2,1,0:T(8,128)S(1)}, u32[]{:S(2)}, u32[]{:S(2)}) collective-permute-start(f32[2,8,512]{2,1,0:T(8,128)S(1)} %copy-done.18), channel_id=1, source_target_pairs={{0,12},{1,13},{2,14},{3,15},{4,0},{5,1},{6,2},{7,3},{8,4},{9,5},{1... | collective-permute-start | bytes 98312 | tf_op jit(solution)/shard_map/ppermute | solution.py:288
  109.3 12.4 %copy-start.9 = (f32[256]{0:T(256)S(1)}, f32[256]{0:T(256)}, u32[]{:S(2)}) copy-start(f32[256]{0:T(256)} %copy-done.8) | copy-start | bytes 3076
  109.3 13.1 %copy-start.17 = (s32[2]{0:T(128)S(1)}, s32[2]{0:T(128)}, u32[]{:S(2)}) copy-start(s32[2]{0:T(128)} %get-tuple-element.54) | copy-start | bytes 28
  109.3 37.9 %collective-permute-start.4 = (bf16[2,256,512]{2,1,0:T(8,128)(2,1)}, bf16[2,256,512]{2,1,0:T(8,128)(2,1)S(1)}, u32[]{:S(2)}, u32[]{:S(2)}) collective-permute-start(bf16[2,256,512]{2,1,0:T(8,128)(2,1)} %get-tuple-element.16), channel_id=1, source_target_pairs={{0,8},{1,9},{2,10},{3,11},{4,12},{5,13},{6,14},{7,15},{8,0},{9,1},... | collective-permute-start | bytes 1572872 | tf_op jit(solution)/shard_map/ppermute | solution.py:288
  120.7 17.6 %collective-permute-start.8 = (f32[2,8,512]{2,1,0:T(8,128)}, f32[2,8,512]{2,1,0:T(8,128)S(1)}, u32[]{:S(2)}, u32[]{:S(2)}) collective-permute-start(f32[2,8,512]{2,1,0:T(8,128)} %get-tuple-element.21), channel_id=1, source_target_pairs={{0,4},{1,5},{2,6},{3,7},{4,8},{5,9},{6,10},{7,11},{8,12},{9,13},{1... | collective-permute-start | bytes 98312 | tf_op jit(solution)/shard_map/ppermute | solution.py:288
  120.8 26.4 %collective-permute-start.5 = (bf16[2,256,512]{2,1,0:T(8,128)(2,1)}, bf16[2,256,512]{2,1,0:T(8,128)(2,1)S(1)}, u32[]{:S(2)}, u32[]{:S(2)}) collective-permute-start(bf16[2,256,512]{2,1,0:T(8,128)(2,1)} %get-tuple-element.17), channel_id=1, source_target_pairs={{0,4},{1,5},{2,6},{3,7},{4,8},{5,9},{6,10},{7,11},{8,12},{9,13},{1... | collective-permute-start | bytes 1572872 | tf_op jit(solution)/shard_map/ppermute | solution.py:288
  124.3 22.9 %copy-start.6 = (bf16[2,256,512]{2,1,0:T(8,128)(2,1)S(1)}, bf16[2,256,512]{2,1,0:T(8,128)(2,1)}, u32[]{:S(2)}) copy-start(bf16[2,256,512]{2,1,0:T(8,128)(2,1)} %copy-done.5) | copy-start | bytes 1572868
  149.3 5.7 %copy-start.7 = (bf16[256,256]{1,0:T(8,128)(2,1)S(1)}, bf16[256,256]{1,0:T(8,128)(2,1)}, u32[]{:S(2)}) copy-start(bf16[256,256]{1,0:T(8,128)(2,1)} %multiply_convert_fusion.1) | copy-start | bytes 393220
  152.9 6.7 %collective-permute-start.9 = (bf16[256,2048]{1,0:T(8,128)(2,1)S(1)}, bf16[256,2048]{1,0:T(8,128)(2,1)}, u32[]{:S(2)}, u32[]{:S(2)}) collective-permute-start(bf16[256,2048]{1,0:T(8,128)(2,1)S(1)} %convolution_convert_fusion), channel_id=1, source_target_pairs={{0,16},{16,0},{1,17},{17,1},{2,18},{18,2},{3,19},{19,3},{4,20},{20... | collective-permute-start | bytes 3145736 | tf_op jit(solution)/shard_map/ppermute | solution.py:429
  (8 other events, 13.7 us)
